TPU v7x, 32 devices: a whole 2x2x4 slice. The times are simulated.
32 devices in a mesh: grp: 2 (over y), seq: 4 (over z), head: 4 (over x, core).
Axes of the slice: x: 2, y: 2, z: 4, core: 2. Of those that a mesh axis runs over, the one named last changes fastest.
Arguments:
- byte_ids: int32 [16384], P(('grp', 'seq')), parts along dimension 0, may hold values from 0 to 255, as said below
- queries: bfloat16 [4, 64, 16384], P('head', None, ('grp', 'seq')), parts along dimension 2, may hold values from -170 to 170
- key_states: bfloat16 [4, 64, 16384], P('head', None, ('grp', 'seq')), parts along dimension 2, may hold values from -12 to 12
- values: bfloat16 [4, 64, 16384], P('head', None, ('grp', 'seq')), parts along dimension 2, may hold values from -10 to 10
- cotangent: bfloat16 [4, 64, 16384], P('head', None, ('grp', 'seq')), parts along dimension 2, may hold values from -10 to 10
Outputs:
- attended: bfloat16 [4, 64, 16384], P('head', None, ('grp', 'seq')), parts along dimension 2
- grad_queries: bfloat16 [4, 64, 16384], P('head', None, ('grp', 'seq')), parts along dimension 2
- grad_keys: bfloat16 [4, 64, 16384], P('head', None, ('grp', 'seq')), parts along dimension 2
- grad_values: bfloat16 [4, 64, 16384], P('head', None, ('grp', 'seq')), parts along dimension 2
There are 2 independent parts, one for each index of `grp`. A program takes and returns all parts, laid end to end along the dimension named above; each array names one. Nothing has to cross between parts.
Inputs may be any that keep to these rules, and one draw needn't show every extreme that they name: `byte_ids`: 0 marks a dropped byte, which is attended only by its own position.
All inputs are finite; a program needn't handle non-finite values.
Results may differ from a plain program's by a relative error of at most 0.0055.
Values sent between devices are 32-bit elements; how exact they have to be, the bound alone decides.
A program may use at most 64 MiB of HBM per device.

v0:
```python
import jax
import jax.numpy as jnp
from jax import lax
from jax.experimental import pallas as pl
from jax.experimental.pallas import tpu as pltpu
from jax.sharding import PartitionSpec as P

HEAD = 64
BLOCK = 128
SPAN = 256
NEAR_DEAD = -(2.0**96)
FAR_DEAD = -(2.0**90)
F32 = jnp.float32
BF16 = jnp.bfloat16


def nn(a, b):
    return lax.dot_general(a, b, (((1,), (0,)), ((), ())), preferred_element_type=F32)


def nt(a, b):
    return lax.dot_general(a, b, (((1,), (1,)), ((), ())), preferred_element_type=F32)


def tn(a, b):
    return lax.dot_general(a, b, (((0,), (0,)), ((), ())), preferred_element_type=F32)


def split(x):
    high = x.astype(BF16)
    return high, (x - high.astype(F32)).astype(BF16)


def iota(shape, dim):
    return lax.broadcasted_iota(jnp.int32, shape, dim)


def pool_matrix(rows, level):
    shape = (rows, rows << level)
    return jnp.where(iota(shape, 1) // (1 << level) == iota(shape, 0), 1.0, 0.0)


def pool_rows(x, level):
    mat = pool_matrix(x.shape[0] >> level, level).astype(BF16)
    high, low = split(x)
    return nn(mat, high) + nn(mat, low)


def spread_rows(x, level):
    mat = pool_matrix(x.shape[0], level).astype(BF16)
    high, low = split(x)
    return tn(mat, high) + tn(mat, low)


def low_lanes(shape):
    return iota(shape, 1) < HEAD


def key_side(kv, count):
    low = low_lanes(kv.shape)
    mean = pltpu.roll(kv / jnp.maximum(count, 1.0), HEAD, 1)
    mean_only = jnp.where(low, 0.0, mean)
    full = jnp.where(low, jnp.where(count > 0, 0.0, FAR_DEAD), mean)
    return full, mean_only


def value_side(kv, count):
    return jnp.where(low_lanes(kv.shape), count, kv)


def query_side(cq, scale):
    return jnp.where(low_lanes(cq.shape), 1.0, cq * scale)


def product3(a, b):
    ah, al = split(a)
    bh, bl = split(b)
    return nt(
        jnp.concatenate([ah, ah, al], axis=1), jnp.concatenate([bh, bl, bh], axis=1)
    )


def far_forward(query, key_full, value):
    scores = product3(query, key_full)
    top = jnp.max(scores, axis=1, keepdims=True)
    high, low = split(top)
    top = high.astype(F32) + low.astype(F32)
    weights = jnp.exp(scores - top).astype(BF16)
    vh, vl = split(value)
    out = nn(jnp.concatenate([weights, weights], axis=1), jnp.concatenate([vh, vl], axis=0))
    return weights, jnp.where(iota(out.shape, 1) == 0, top, out)


def far_backward(query, key_mean, value, count, weights, row_grad, scale):
    inner = product3(row_grad, value)
    dscore = (weights.astype(F32) * inner).astype(BF16)
    grad_query = nn(dscore, key_mean.astype(BF16)) * scale
    dk = tn(dscore, query.astype(BF16))
    dv = tn(weights, row_grad.astype(BF16))
    dk = pltpu.roll(dk, HEAD, 1) / jnp.maximum(count, 1.0)
    return grad_query, jnp.where(low_lanes(dv.shape), dk, dv)


def kernel(size, refs):
    bits = size.bit_length() - 1
    it = iter(refs)
    ids, q_ref, k_ref, v_ref, g_ref = (next(it) for _ in range(5))
    att_ref, gq_ref, gk_ref, gv_ref = (next(it) for _ in range(4))
    pall, kv_s, cq_s, wn_s, num_s, top_s, wf_s, fh_s, fl_s, rg_s = (next(it) for _ in range(10))
    gain_s, stat_s, sc_s, dq_s, dkv_s, dv_s = (next(it) for _ in range(6))
    sends = [next(it) for _ in range(bits)]
    recvs = [next(it) for _ in range(bits)]
    back_sends = [next(it) for _ in range(bits)]
    back_recvs = [next(it) for _ in range(bits)]
    send_sem, recv_sem, back_send_sem, back_recv_sem = (next(it) for _ in range(4))

    tokens = q_ref.shape[2]
    chunks = tokens // SPAN
    local_top = (tokens // BLOCK).bit_length() - 1
    scale = HEAD**-0.5
    me = lax.axis_index("seq")

    def flipped(m):
        out = me
        for bit in range(bits):
            if m >> bit & 1:
                out = out + (1 - 2 * lax.rem(lax.div(me, 1 << bit), 2)) * (1 << bit)
        return out

    barrier = pltpu.get_barrier_semaphore()
    for m in range(1, size):
        pl.semaphore_signal(
            barrier, inc=1, device_id={"seq": flipped(m)}, device_id_type=pl.DeviceIdType.MESH
        )

    start = {}
    at = 0
    for level in range(1, local_top + 1):
        start[level] = at
        at += tokens >> level
    prow = {}
    at = 0
    for level in range(1, local_top + 1):
        prow[level] = at
        at += SPAN >> level
    pooled_rows = at

    pieces = [pool_matrix(SPAN >> level, level) for level in range(1, local_top + 1)]
    pieces.append(jnp.zeros((SPAN - pooled_rows, SPAN), F32))
    pall[...] = jnp.concatenate(pieces, axis=0).astype(BF16)

    def span(p):
        return pl.ds(p * SPAN, SPAN)

    def level_rows(p, level):
        n = SPAN >> level
        return pl.ds(start[level] + p * n, n)

    def pool_slice(level):
        return pl.ds(prow[level], SPAN >> level)

    for p in range(chunks):
        cols = span(p)
        mask = jnp.where(ids[:, cols] != 0, 1.0, 0.0)
        maskh = jnp.broadcast_to(mask, (HEAD, SPAN))
        km = (k_ref[0, :, cols].astype(F32) * maskh).astype(BF16)
        vm = (v_ref[0, :, cols].astype(F32) * maskh).astype(BF16)
        x = jnp.concatenate([km, vm, maskh.astype(BF16), q_ref[0, :, cols]], axis=0)
        r = nt(pall[...], x)
        for level in range(1, local_top + 1):
            piece = r[prow[level] : prow[level] + (SPAN >> level)]
            kv_s[level_rows(p, level), :] = piece[:, :128]
            cq_s[level_rows(p, level), :] = piece[:, 128:]

    kv = kv_s[pl.ds(start[local_top], BLOCK), :]
    cq = cq_s[pl.ds(start[local_top], BLOCK), :]
    cross_query = []
    for b in range(bits):
        if b:
            kv, cq = pool_rows(kv, 1), pool_rows(cq, 1)
        cross_query.append(query_side(cq, scale * 2.0 ** -(local_top + b)))
        rows = BLOCK >> b
        sends[b][pl.ds(0, rows), :] = kv
        wide = cq if not b else jnp.concatenate([cq, jnp.zeros((BLOCK - rows, 128), F32)], axis=0)
        sends[b][pl.ds(rows, 8), :] = wide.T[:8]

    pl.semaphore_wait(barrier, size - 1)
    copies = []
    for m in range(1, size):
        b = m.bit_length() - 1
        copy = pltpu.make_async_remote_copy(
            src_ref=sends[b],
            dst_ref=recvs[b].at[lax.rem(me, 1 << b)],
            send_sem=send_sem.at[m - 1],
            recv_sem=recv_sem.at[m - 1],
            device_id={"seq": flipped(m)},
            device_id_type=pl.DeviceIdType.MESH,
        )
        copy.start()
        copies.append(copy)

    eye = iota((SPAN, SPAN), 0) == iota((SPAN, SPAN), 1)
    first = iota((16, SPAN), 0) == 0
    ones16 = jnp.where(first, 1.0, 0.0).astype(BF16)
    for p in range(chunks):
        cols = span(p)
        q = q_ref[0, :, cols]
        k = k_ref[0, :, cols]
        dead = jnp.where(ids[:, cols] != 0, 0.0, NEAR_DEAD)
        dead = jnp.where(first, dead, 0.0).astype(BF16)
        qf = q.astype(F32) * scale
        own = jnp.sum(qf * k.astype(F32), axis=0, keepdims=True)
        scores = tn(
            jnp.concatenate([k, dead], axis=0), jnp.concatenate([qf.astype(BF16), ones16], axis=0)
        )
        scores = jnp.where(eye, own, scores)
        top = jnp.max(scores, axis=0, keepdims=True)
        w = jnp.exp(scores - top).astype(BF16)
        wn_s[p] = w
        num_s[:, cols] = nn(jnp.concatenate([v_ref[0, :, cols], ones16], axis=0), w)
        top_s[:, cols] = jnp.broadcast_to(top, (8, SPAN))

    def far_operands(level, g):
        own = pl.ds(start[level] + g * BLOCK, BLOCK)
        other = pl.ds(start[level] + (g ^ 1) * BLOCK, BLOCK)
        kv = kv_s[other, :]
        count = cq_s[other, :]
        query = query_side(cq_s[own, :], scale * 2.0**-level)
        return own, other, kv, count, query

    for level in range(1, local_top):
        for g in range((tokens >> level) // BLOCK):
            own, other, kv, count, query = far_operands(level, g)
            w, f = far_forward(query, key_side(kv, count)[0], value_side(kv, count))
            wf_s[own, :] = w
            fh_s[own, :], fl_s[own, :] = split(f)

    for copy in copies:
        copy.wait_recv()
    cross = []
    for b in range(bits):
        rows = BLOCK >> b
        parts = [recvs[b][s] for s in range(1 << b)]
        kv = jnp.concatenate([x[:rows] for x in parts], axis=0)
        counts = []
        for x in parts:
            tile = jnp.concatenate([x[rows:]] * (BLOCK // 8), axis=0).T
            counts.append(tile[:rows])
        count = jnp.concatenate(counts, axis=0)
        key_full, key_mean = key_side(kv, count)
        value = value_side(kv, count)
        w, f = far_forward(cross_query[b], key_full, value)
        if b:
            f = spread_rows(f, b)
        cross.append((key_mean, value, count, w, f))
    best = cross[0][4][:, :1]
    for b in range(1, bits):
        best = jnp.maximum(best, cross[b][4][:, :1])
    gains = [jnp.exp(c[4][:, :1] - best) for c in cross]
    total = gains[0] * cross[0][4]
    for b in range(1, bits):
        total = total + gains[b] * cross[b][4]
    total = jnp.where(iota(total.shape, 1) == 0, best, total)
    whole = pl.ds(start[local_top], BLOCK)
    fh_s[whole, :], fl_s[whole, :] = split(total)

    row64 = iota((HEAD, SPAN), 0)
    for p in range(chunks):
        cols = span(p)
        wide = []
        for level in range(1, local_top + 1):
            rows = level_rows(p, level)
            mat = pall[pool_slice(level), :]
            wide.append(
                tn(
                    jnp.concatenate([fh_s[rows, :], fl_s[rows, :]], axis=0),
                    jnp.concatenate([mat, mat], axis=0),
                )
            )
        near_top = top_s[:1, cols]
        row_top = near_top
        for x in wide:
            row_top = jnp.maximum(row_top, x[:1])
        near_factor = jnp.exp(near_top - row_top)
        near = num_s[:, cols]
        numer = near_factor * near[:HEAD]
        denom = near_factor * near[HEAD : HEAD + 1]
        factors = []
        for x in wide:
            factor = jnp.exp(x[:1] - row_top)
            factors.append(factor)
            numer = numer + factor * x[HEAD:]
            denom = denom + factor * x[1:2]
        inverse = 1.0 / denom
        output = numer * inverse
        att_ref[0, :, cols] = output.astype(BF16)
        g = g_ref[0, :, cols].astype(F32)
        stat = jnp.sum(g * output, axis=0, keepdims=True)
        gain = near_factor * inverse
        gain_s[:, cols] = jnp.broadcast_to(gain, (8, SPAN))
        stat_s[:, cols] = jnp.broadcast_to(stat, (8, SPAN))
        sc_s[:, cols] = (gain * g).astype(BF16)
        for level in range(1, local_top + 1):
            far_gain = factors[level - 1] * inverse
            down = -(far_gain * stat)
            high = down.astype(BF16).astype(F32)
            head = jnp.where(row64 == 0, high, jnp.where(row64 == 1, down - high, 0.0))
            x = jnp.concatenate([head.astype(BF16), (far_gain * g).astype(BF16)], axis=0)
            rg_s[level_rows(p, level), :] = nt(pall[pool_slice(level), :], x)

    base = rg_s[whole, :]
    dq_total = None
    for b in range(bits):
        key_mean, value, count, w, _ = cross[b]
        row_grad = base * gains[b]
        if b:
            row_grad = pool_rows(row_grad, b)
        dq, dkv = far_backward(
            cross_query[b], key_mean, value, count, w, row_grad, scale * 2.0 ** -(local_top + b)
        )
        rows = BLOCK >> b
        for s in range(1 << b):
            back_sends[b][s] = dkv[s * rows : (s + 1) * rows]
        if b:
            dq = spread_rows(dq, b)
        dq_total = dq if dq_total is None else dq_total + dq
    dq_s[whole, :] = dq_total.astype(BF16)
    back_copies = []
    for m in range(1, size):
        b = m.bit_length() - 1
        copy = pltpu.make_async_remote_copy(
            src_ref=back_sends[b].at[lax.rem(flipped(m), 1 << b)],
            dst_ref=back_recvs[b].at[lax.rem(me, 1 << b)],
            send_sem=back_send_sem.at[m - 1],
            recv_sem=back_recv_sem.at[m - 1],
            device_id={"seq": flipped(m)},
            device_id_type=pl.DeviceIdType.MESH,
        )
        copy.start()
        back_copies.append(copy)

    for level in range(1, local_top):
        for g in range((tokens >> level) // BLOCK):
            own, other, kv, count, query = far_operands(level, g)
            dq, dkv = far_backward(
                query,
                key_side(kv, count)[1],
                value_side(kv, count),
                count,
                wf_s[own, :],
                rg_s[own, :],
                scale * 2.0**-level,
            )
            dq_s[own, :] = dq.astype(BF16)
            dkv_s[other, :] = dkv.astype(BF16)

    for p in range(chunks):
        cols = span(p)
        q, k, v, g = (r[0, :, cols] for r in (q_ref, k_ref, v_ref, g_ref))
        w = wn_s[p]
        dprob = tn(v, g)
        dscore = (
            w.astype(F32) * gain_s[:1, cols] * (dprob - stat_s[:1, cols])
        ).astype(BF16)
        num_s[:HEAD, cols] = nt(q, dscore) * scale
        dv_s[:, cols] = nt(sc_s[:, cols], w)
        gq = nn(k, dscore) * scale
        rows = [level_rows(p, level) for level in range(1, local_top + 1)]
        pad = jnp.zeros((SPAN - pooled_rows, 128), BF16)
        d = jnp.concatenate([dq_s[r, :] for r in rows] + [pad], axis=0)
        gq_ref[0, :, cols] = (gq + tn(d, pall[...])[HEAD:]).astype(BF16)

    for copy in back_copies:
        copy.wait_recv()
    acc = None
    for b in reversed(range(bits)):
        if acc is not None:
            acc = spread_rows(acc, 1)
        for s in range(1 << b):
            acc = back_recvs[b][s] if acc is None else acc + back_recvs[b][s]
    dkv_s[whole, :] = acc.astype(BF16)
    for p in range(chunks):
        cols = span(p)
        rows = [level_rows(p, level) for level in range(1, local_top + 1)]
        pad = jnp.zeros((SPAN - pooled_rows, 128), BF16)
        d = jnp.concatenate([dkv_s[r, :] for r in rows] + [pad], axis=0)
        far = tn(d, pall[...])
        valid = ids[:, cols] != 0
        far = jnp.where(valid, far, 0.0)
        gk_ref[0, :, cols] = (num_s[:HEAD, cols] + far[:HEAD]).astype(BF16)
        gv_ref[0, :, cols] = (dv_s[:, cols] + far[HEAD:]).astype(BF16)
    for copy in copies + back_copies:
        copy.wait_send()


def local(byte_ids, queries, key_states, values, cotangent):
    heads, width, tokens = queries.shape
    size = lax.axis_size("seq")
    bits = size.bit_length() - 1
    chunks = tokens // SPAN
    coarse = tokens - (tokens >> ((tokens // BLOCK).bit_length() - 1))
    vmem = pltpu.VMEM
    scratch = [
        vmem((SPAN, SPAN), BF16),
        vmem((coarse, 128), F32),
        vmem((coarse, 128), F32),
        vmem((chunks, SPAN, SPAN), BF16),
        vmem((HEAD + 16, tokens), F32),
        vmem((8, tokens), F32),
        vmem((coarse, 128), BF16),
        vmem((coarse, 128), BF16),
        vmem((coarse, 128), BF16),
        vmem((coarse, 128), F32),
        vmem((8, tokens), F32),
        vmem((8, tokens), F32),
        vmem((HEAD, tokens), BF16),
        vmem((coarse, 128), BF16),
        vmem((coarse, 128), BF16),
        vmem((HEAD, tokens), F32),
    ]
    scratch += [vmem(((BLOCK >> b) + 8, 128), F32) for b in range(bits)]
    scratch += [vmem((1 << b, (BLOCK >> b) + 8, 128), F32) for b in range(bits)]
    scratch += [vmem((1 << b, BLOCK >> b, 128), F32) for b in range(bits)] * 2
    scratch += [pltpu.SemaphoreType.DMA((size - 1,))] * 4
    out = jax.ShapeDtypeStruct(queries.shape, BF16)
    return pl.pallas_call(
        lambda *refs: kernel(size, refs),
        out_shape=(out,) * 4,
        in_specs=[pl.BlockSpec(memory_space=pltpu.VMEM)] * 5,
        out_specs=(pl.BlockSpec(memory_space=pltpu.VMEM),) * 4,
        scratch_shapes=scratch,
        compiler_params=pltpu.CompilerParams(
            collective_id=0, has_side_effects=True, vmem_limit_bytes=40 * 2**20
        ),
        cost_estimate=pl.CostEstimate(
            flops=2 * 10**9, bytes_accessed=3 * 10**6, transcendentals=10**6
        ),
    )(byte_ids.reshape(1, tokens), queries, key_states, values, cotangent)


def solution(mesh):
    wide = P("head", None, ("grp", "seq"))
    return jax.shard_map(
        local,
        mesh=mesh,
        in_specs=(P(("grp", "seq")), wide, wide, wide, wide),
        out_specs=(wide,) * 4,
        check_vma=False,
    )
```

profile of v0, /device:TPU:0, one launch (start us, length us, event | category | flops | bytes accessed | tf_op | source)
XLA Modules:
  0.0 29.6 jit_solution(16799484571327630793)
XLA Ops:
  0.6 0.0 copy-start
  0.6 0.9 %copy-done = bf16[1,64,2048]{2,1,0:T(8,128)(2,1)S(1)} copy-done((bf16[1,64,2048]{2,1,0:T(8,128)(2,1)S(1)}, bf16[1,64,2048]{2,1,0:T(8,128)(2,1)}, u32[]{:S(2)}) %copy-start) | copy-done | bytes 262168
  1.6 0.0 copy-start.1
  1.6 0.9 %copy-done.1 = bf16[1,64,2048]{2,1,0:T(8,128)(2,1)S(1)} copy-done((bf16[1,64,2048]{2,1,0:T(8,128)(2,1)S(1)}, bf16[1,64,2048]{2,1,0:T(8,128)(2,1)}, u32[]{:S(2)}) %copy-start.1) | copy-done | bytes 262168
  2.5 0.0 copy-start.2
  2.5 0.9 %copy-done.2 = bf16[1,64,2048]{2,1,0:T(8,128)(2,1)S(1)} copy-done((bf16[1,64,2048]{2,1,0:T(8,128)(2,1)S(1)}, bf16[1,64,2048]{2,1,0:T(8,128)(2,1)}, u32[]{:S(2)}) %copy-start.2) | copy-done | bytes 262168
  3.5 0.0 copy-start.3
  3.5 0.9 %copy-done.3 = bf16[1,64,2048]{2,1,0:T(8,128)(2,1)S(1)} copy-done((bf16[1,64,2048]{2,1,0:T(8,128)(2,1)S(1)}, bf16[1,64,2048]{2,1,0:T(8,128)(2,1)}, u32[]{:S(2)}) %copy-start.3) | copy-done | bytes 262168
  4.4 0.0 copy-start.4
  4.4 0.7 %copy-done.4 = s32[2048]{0:T(1024)S(1)} copy-done((s32[2048]{0:T(1024)S(1)}, s32[2048]{0:T(1024)}, u32[]{:S(2)}) %copy-start.4) | copy-done | bytes 8216
  5.1 21.7 %shard_map.84 = (bf16[1,64,2048]{2,1,0:T(8,128)(2,1)S(1)}, bf16[1,64,2048]{2,1,0:T(8,128)(2,1)S(1)}, bf16[1,64,2048]{2,1,0:T(8,128)(2,1)S(1)}, bf16[1,64,2048]{2,1,0:T(8,128)(2,1)S(1)}) custom-call(s32[1,2048]{1,0:T(1,128)S(1)} %bitcast.1, bf16[1,64,2048]{2,1,0:T(8,128)(2,1)S(1)} %copy-done, bf16[1,64,2048]{2,1,0:T(8,128)(2,1)S(1)} %copy-done.1, ...), custom_call_target="tpu_custom_call" | custom-call | flops 2000000000 | bytes 3000000 | tf_op jit(solution)/shard_map/pallas_call | solution.py:426
  26.8 0.7 %copy.13 = bf16[1,64,2048]{2,1,0:T(8,128)(2,1)} copy(bf16[1,64,2048]{2,1,0:T(8,128)(2,1)S(1)} %get-tuple-element.8) | data formatting | bytes 524288
  27.5 0.7 %copy.14 = bf16[1,64,2048]{2,1,0:T(8,128)(2,1)} copy(bf16[1,64,2048]{2,1,0:T(8,128)(2,1)S(1)} %get-tuple-element.9) | data formatting | bytes 524288
  28.2 0.7 %copy.15 = bf16[1,64,2048]{2,1,0:T(8,128)(2,1)} copy(bf16[1,64,2048]{2,1,0:T(8,128)(2,1)S(1)} %get-tuple-element.10) | data formatting | bytes 524288
  28.9 0.7 %copy.16 = bf16[1,64,2048]{2,1,0:T(8,128)(2,1)} copy(bf16[1,64,2048]{2,1,0:T(8,128)(2,1)S(1)} %get-tuple-element.11) | data formatting | bytes 524288
Async XLA Ops:
  0.6 1.0 %copy-start = (bf16[1,64,2048]{2,1,0:T(8,128)(2,1)S(1)}, bf16[1,64,2048]{2,1,0:T(8,128)(2,1)}, u32[]{:S(2)}) copy-start(bf16[1,64,2048]{2,1,0:T(8,128)(2,1)} %refs_1_.1) | copy-start | bytes 786436
  1.6 0.9 %copy-start.1 = (bf16[1,64,2048]{2,1,0:T(8,128)(2,1)S(1)}, bf16[1,64,2048]{2,1,0:T(8,128)(2,1)}, u32[]{:S(2)}) copy-start(bf16[1,64,2048]{2,1,0:T(8,128)(2,1)} %refs_2_.1) | copy-start | bytes 786436
  2.5 0.9 %copy-start.2 = (bf16[1,64,2048]{2,1,0:T(8,128)(2,1)S(1)}, bf16[1,64,2048]{2,1,0:T(8,128)(2,1)}, u32[]{:S(2)}) copy-start(bf16[1,64,2048]{2,1,0:T(8,128)(2,1)} %refs_3_.1) | copy-start | bytes 786436
  3.5 0.9 %copy-start.3 = (bf16[1,64,2048]{2,1,0:T(8,128)(2,1)S(1)}, bf16[1,64,2048]{2,1,0:T(8,128)(2,1)}, u32[]{:S(2)}) copy-start(bf16[1,64,2048]{2,1,0:T(8,128)(2,1)} %refs_4_.1) | copy-start | bytes 786436
  4.4 0.7 %copy-start.4 = (s32[2048]{0:T(1024)S(1)}, s32[2048]{0:T(1024)}, u32[]{:S(2)}) copy-start(s32[2048]{0:T(1024)} %param.5) | copy-start | bytes 24580
where the time goes:
time: 29.9 us; the launch traced here: 29.6 us
  Pallas kernels  21.7 us (73%)
  local copies, waits for them, and re-layouts  7.3 us (24%)
  between operations  0.65 us (2%)
    pallas_call x1, Pallas kernels, local(): pl.pallas_call(lambda *refs: kernel(size, refs), out_shape=(out,) * 4, in...  21.7 us
    unnamed x14, local copies, waits for them, and re-layouts  7.3 us

commit v1 on v0

--- a/solution.py
+++ b/solution.py
@@ -6,6 +6,7 @@
 from jax.sharding import PartitionSpec as P
 
 HEAD = 64
+VMEM_LIMIT = 62 * 2**20
 BLOCK = 128
 SPAN = 256
 NEAR_DEAD = -(2.0**96)
@@ -104,8 +105,8 @@
 def kernel(size, refs):
     bits = size.bit_length() - 1
     it = iter(refs)
-    ids, q_ref, k_ref, v_ref, g_ref = (next(it) for _ in range(5))
-    att_ref, gq_ref, gk_ref, gv_ref = (next(it) for _ in range(4))
+    sources = [next(it) for _ in range(5)]
+    targets = [next(it) for _ in range(4)]
     pall, kv_s, cq_s, wn_s, num_s, top_s, wf_s, fh_s, fl_s, rg_s = (next(it) for _ in range(10))
     gain_s, stat_s, sc_s, dq_s, dkv_s, dv_s = (next(it) for _ in range(6))
     sends = [next(it) for _ in range(bits)]
@@ -113,6 +114,13 @@
     back_sends = [next(it) for _ in range(bits)]
     back_recvs = [next(it) for _ in range(bits)]
     send_sem, recv_sem, back_send_sem, back_recv_sem = (next(it) for _ in range(4))
+    ids, q_ref, k_ref, v_ref, g_ref = held = [next(it) for _ in range(5)]
+    att_ref, gq_ref, gk_ref, gv_ref = results = [next(it) for _ in range(4)]
+    in_sem, out_sem = next(it), next(it)
+    stores = [pltpu.make_async_copy(x, y, out_sem.at[i]) for i, (x, y) in enumerate(zip(results, targets))]
+    loads = [pltpu.make_async_copy(x, y, in_sem.at[i]) for i, (x, y) in enumerate(zip(sources, held))]
+    for i in (0, 2, 3, 1, 4):
+        loads[i].start()
 
     tokens = q_ref.shape[2]
     chunks = tokens // SPAN
@@ -158,6 +166,9 @@
 
     def pool_slice(level):
         return pl.ds(prow[level], SPAN >> level)
+
+    for i in range(4):
+        loads[i].wait()
 
     for p in range(chunks):
         cols = span(p)
@@ -263,6 +274,8 @@
     total = jnp.where(iota(total.shape, 1) == 0, best, total)
     whole = pl.ds(start[local_top], BLOCK)
     fh_s[whole, :], fl_s[whole, :] = split(total)
+
+    loads[4].wait()
 
     row64 = iota((HEAD, SPAN), 0)
     for p in range(chunks):
@@ -308,6 +321,8 @@
             x = jnp.concatenate([head.astype(BF16), (far_gain * g).astype(BF16)], axis=0)
             rg_s[level_rows(p, level), :] = nt(pall[pool_slice(level), :], x)
 
+    stores[0].start()
+
     base = rg_s[whole, :]
     dq_total = None
     for b in range(bits):
@@ -370,6 +385,7 @@
         d = jnp.concatenate([dq_s[r, :] for r in rows] + [pad], axis=0)
         gq_ref[0, :, cols] = (gq + tn(d, pall[...])[HEAD:]).astype(BF16)
 
+    stores[1].start()
     for copy in back_copies:
         copy.wait_recv()
     acc = None
@@ -389,8 +405,21 @@
         far = jnp.where(valid, far, 0.0)
         gk_ref[0, :, cols] = (num_s[:HEAD, cols] + far[:HEAD]).astype(BF16)
         gv_ref[0, :, cols] = (dv_s[:, cols] + far[HEAD:]).astype(BF16)
+    stores[2].start()
+    stores[3].start()
     for copy in copies + back_copies:
         copy.wait_send()
+    for store in stores:
+        store.wait()
+
+
+def flush(*refs):
+    sem = refs[8]
+    copies = [pltpu.make_async_copy(refs[i], refs[4 + i], sem.at[i]) for i in range(4)]
+    for copy in copies:
+        copy.start()
+    for copy in copies:
+        copy.wait()
 
 
 def local(byte_ids, queries, key_states, values, cotangent):
@@ -422,20 +451,30 @@
     scratch += [vmem((1 << b, (BLOCK >> b) + 8, 128), F32) for b in range(bits)]
     scratch += [vmem((1 << b, BLOCK >> b, 128), F32) for b in range(bits)] * 2
     scratch += [pltpu.SemaphoreType.DMA((size - 1,))] * 4
+    scratch += [vmem((1, tokens), jnp.int32)] + [vmem(queries.shape, BF16)] * 8
+    scratch += [pltpu.SemaphoreType.DMA((5,)), pltpu.SemaphoreType.DMA((4,))]
     out = jax.ShapeDtypeStruct(queries.shape, BF16)
-    return pl.pallas_call(
+    results = pl.pallas_call(
         lambda *refs: kernel(size, refs),
         out_shape=(out,) * 4,
-        in_specs=[pl.BlockSpec(memory_space=pltpu.VMEM)] * 5,
-        out_specs=(pl.BlockSpec(memory_space=pltpu.VMEM),) * 4,
+        in_specs=[pl.BlockSpec(memory_space=pltpu.HBM)] * 5,
+        out_specs=(pl.BlockSpec(memory_space=pltpu.HBM),) * 4,
         scratch_shapes=scratch,
         compiler_params=pltpu.CompilerParams(
-            collective_id=0, has_side_effects=True, vmem_limit_bytes=40 * 2**20
+            collective_id=0, has_side_effects=True, vmem_limit_bytes=VMEM_LIMIT
         ),
         cost_estimate=pl.CostEstimate(
             flops=2 * 10**9, bytes_accessed=3 * 10**6, transcendentals=10**6
         ),
     )(byte_ids.reshape(1, tokens), queries, key_states, values, cotangent)
+    return pl.pallas_call(
+        flush,
+        out_shape=(out,) * 4,
+        in_specs=[pl.BlockSpec(memory_space=pltpu.HBM)] * 4,
+        out_specs=(pl.BlockSpec(memory_space=pltpu.HBM),) * 4,
+        scratch_shapes=[pltpu.SemaphoreType.DMA((4,))],
+        compiler_params=pltpu.CompilerParams(vmem_limit_bytes=VMEM_LIMIT),
+    )(*results)
 
 
 def solution(mesh):

time: 29.9 us -> 56.4 us (1.89)
  Pallas kernels: 21.7 us -> 55.6 us
  local copies, waits for them, and re-layouts: 7.3 us -> 0 us
    pallas_call x0 -> x1, Pallas kernels: none -> 32.9 us  [local(): pl.pallas_call(flush, out_shape=(out,) * 4, in_specs=[pl.BlockSpec(memory...]
    unnamed x14 -> x0, local copies, waits for them, and re-layouts: 7.3 us -> none
    pallas_call x1, Pallas kernels: 21.7 us -> 22.7 us  [local(): pl.pallas_call(lambda *refs: kernel(size, refs), out_shape=(out,) * 4, in...]
where the time goes in v1:
time: 56.4 us; the launch traced here: 56.2 us
  Pallas kernels  55.6 us (99%)
  between operations  0.64 us (1%)
    pallas_call x1, Pallas kernels, local(): pl.pallas_call(flush, out_shape=(out,) * 4, in_specs=[pl.BlockSpec(memory...  32.9 us
    pallas_call x1, Pallas kernels, local(): pl.pallas_call(lambda *refs: kernel(size, refs), out_shape=(out,) * 4, in...  22.7 us

profile of v1, /device:TPU:0, one launch (start us, length us, event | category | flops | bytes accessed | tf_op | source)
XLA Modules:
  0.0 56.2 jit_solution(18170305459086303572)
XLA Ops:
  0.6 22.7 %shard_map.84 = (bf16[1,64,2048]{2,1,0:T(8,128)(2,1)}, bf16[1,64,2048]{2,1,0:T(8,128)(2,1)}, bf16[1,64,2048]{2,1,0:T(8,128)(2,1)}, bf16[1,64,2048]{2,1,0:T(8,128)(2,1)}) custom-call(s32[1,2048]{1,0:T(1,128)} %bitcast.1, bf16[1,64,2048]{2,1,0:T(8,128)(2,1)} %refs_1_.1, bf16[1,64,2048]{2,1,0:T(8,128)(2,1)} %refs_2_.1, bf16[1,64,2048]{2,1,0:T(8,128)(2,1)} %refs_3_.1, ...), custom_call_target="tpu_custom_call" | custom-call | flops 2000000000 | bytes 3000000 | tf_op jit(solution)/shard_map/pallas_call | solution.py:457
  23.3 32.9 %shard_map.85 = (bf16[1,64,2048]{2,1,0:T(8,128)(2,1)}, bf16[1,64,2048]{2,1,0:T(8,128)(2,1)}, bf16[1,64,2048]{2,1,0:T(8,128)(2,1)}, bf16[1,64,2048]{2,1,0:T(8,128)(2,1)}) custom-call(bf16[1,64,2048]{2,1,0:T(8,128)(2,1)} %get-tuple-element.8.refs_0_, bf16[1,64,2048]{2,1,0:T(8,128)(2,1)} %get-tuple-element.9.refs_1_, ...), custom_call_target="tpu_custom_call" | custom-call | tf_op jit(solution)/shard_map/pallas_call | solution.py:470

commit v2 on v1

--- a/solution.py
+++ b/solution.py
@@ -414,12 +414,16 @@
 
 
 def flush(*refs):
-    sem = refs[8]
-    copies = [pltpu.make_async_copy(refs[i], refs[4 + i], sem.at[i]) for i in range(4)]
-    for copy in copies:
-        copy.start()
-    for copy in copies:
-        copy.wait()
+    sem = refs[12]
+    loads = [pltpu.make_async_copy(refs[i], refs[8 + i], sem.at[i]) for i in range(4)]
+    stores = [pltpu.make_async_copy(refs[8 + i], refs[4 + i], sem.at[4 + i]) for i in range(4)]
+    for load in loads:
+        load.start()
+    for load, store in zip(loads, stores):
+        load.wait()
+        store.start()
+    for store in stores:
+        store.wait()
 
 
 def local(byte_ids, queries, key_states, values, cotangent):
@@ -472,7 +476,7 @@
         out_shape=(out,) * 4,
         in_specs=[pl.BlockSpec(memory_space=pltpu.HBM)] * 4,
         out_specs=(pl.BlockSpec(memory_space=pltpu.HBM),) * 4,
-        scratch_shapes=[pltpu.SemaphoreType.DMA((4,))],
+        scratch_shapes=[vmem(queries.shape, BF16)] * 4 + [pltpu.SemaphoreType.DMA((8,))],
         compiler_params=pltpu.CompilerParams(vmem_limit_bytes=VMEM_LIMIT),
     )(*results)
 

time: 56.4 us -> 25.5 us (0.45)
  Pallas kernels: 55.6 us -> 24.7 us
    pallas_call x1, Pallas kernels: 32.9 us -> 1.98 us  [local(): pl.pallas_call(flush, out_shape=(out,) * 4, in_specs=[pl.BlockSpec(memory...]
where the time goes in v2:
time: 25.5 us; the launch traced here: 25.3 us
  Pallas kernels  24.7 us (97%)
  between operations  0.64 us (3%)
    pallas_call x1, Pallas kernels, local(): pl.pallas_call(lambda *refs: kernel(size, refs), out_shape=(out,) * 4, in...  22.7 us
    pallas_call x1, Pallas kernels, local(): pl.pallas_call(flush, out_shape=(out,) * 4, in_specs=[pl.BlockSpec(memory...  1.98 us

profile of v2, /device:TPU:0, one launch (start us, length us, event | category | flops | bytes accessed | tf_op | source)
XLA Modules:
  0.0 25.3 jit_solution(13964197254707076705)
XLA Ops:
  0.6 22.7 %shard_map.84 = (bf16[1,64,2048]{2,1,0:T(8,128)(2,1)}, bf16[1,64,2048]{2,1,0:T(8,128)(2,1)}, bf16[1,64,2048]{2,1,0:T(8,128)(2,1)}, bf16[1,64,2048]{2,1,0:T(8,128)(2,1)}) custom-call(s32[1,2048]{1,0:T(1,128)} %bitcast.1, bf16[1,64,2048]{2,1,0:T(8,128)(2,1)} %refs_1_.1, bf16[1,64,2048]{2,1,0:T(8,128)(2,1)} %refs_2_.1, bf16[1,64,2048]{2,1,0:T(8,128)(2,1)} %refs_3_.1, ...), custom_call_target="tpu_custom_call" | custom-call | flops 2000000000 | bytes 3000000 | tf_op jit(solution)/shard_map/pallas_call | solution.py:461
  23.3 2.0 %shard_map.85 = (bf16[1,64,2048]{2,1,0:T(8,128)(2,1)}, bf16[1,64,2048]{2,1,0:T(8,128)(2,1)}, bf16[1,64,2048]{2,1,0:T(8,128)(2,1)}, bf16[1,64,2048]{2,1,0:T(8,128)(2,1)}) custom-call(bf16[1,64,2048]{2,1,0:T(8,128)(2,1)} %get-tuple-element.8.refs_0_, bf16[1,64,2048]{2,1,0:T(8,128)(2,1)} %get-tuple-element.9.refs_1_, ...), custom_call_target="tpu_custom_call" | custom-call | tf_op jit(solution)/shard_map/pallas_call | solution.py:474

commit v3 on v2

--- a/solution.py
+++ b/solution.py
@@ -197,7 +197,7 @@
 
     pl.semaphore_wait(barrier, size - 1)
     copies = []
-    for m in range(1, size):
+    for m in reversed(range(1, size)):
         b = m.bit_length() - 1
         copy = pltpu.make_async_remote_copy(
             src_ref=sends[b],
@@ -246,10 +246,10 @@
             wf_s[own, :] = w
             fh_s[own, :], fl_s[own, :] = split(f)
 
-    for copy in copies:
-        copy.wait_recv()
     cross = []
     for b in range(bits):
+        for m in range(1 << b, 2 << b):
+            copies[size - 1 - m].wait_recv()
         rows = BLOCK >> b
         parts = [recvs[b][s] for s in range(1 << b)]
         kv = jnp.concatenate([x[:rows] for x in parts], axis=0)
@@ -325,7 +325,8 @@
 
     base = rg_s[whole, :]
     dq_total = None
-    for b in range(bits):
+    back_copies = []
+    for b in reversed(range(bits)):
         key_mean, value, count, w, _ = cross[b]
         row_grad = base * gains[b]
         if b:
@@ -336,23 +337,21 @@
         rows = BLOCK >> b
         for s in range(1 << b):
             back_sends[b][s] = dkv[s * rows : (s + 1) * rows]
+        for m in range(1 << b, 2 << b):
+            copy = pltpu.make_async_remote_copy(
+                src_ref=back_sends[b].at[lax.rem(flipped(m), 1 << b)],
+                dst_ref=back_recvs[b].at[lax.rem(me, 1 << b)],
+                send_sem=back_send_sem.at[m - 1],
+                recv_sem=back_recv_sem.at[m - 1],
+                device_id={"seq": flipped(m)},
+                device_id_type=pl.DeviceIdType.MESH,
+            )
+            copy.start()
+            back_copies.append(copy)
         if b:
             dq = spread_rows(dq, b)
         dq_total = dq if dq_total is None else dq_total + dq
     dq_s[whole, :] = dq_total.astype(BF16)
-    back_copies = []
-    for m in range(1, size):
-        b = m.bit_length() - 1
-        copy = pltpu.make_async_remote_copy(
-            src_ref=back_sends[b].at[lax.rem(flipped(m), 1 << b)],
-            dst_ref=back_recvs[b].at[lax.rem(me, 1 << b)],
-            send_sem=back_send_sem.at[m - 1],
-            recv_sem=back_recv_sem.at[m - 1],
-            device_id={"seq": flipped(m)},
-            device_id_type=pl.DeviceIdType.MESH,
-        )
-        copy.start()
-        back_copies.append(copy)
 
     for level in range(1, local_top):
         for g in range((tokens >> level) // BLOCK):

time: 25.5 us -> 25.9 us (1.016)
  Pallas kernels: 24.7 us -> 25 us
    pallas_call x1, Pallas kernels: 22.7 us -> 23 us  [local(): pl.pallas_call(lambda *refs: kernel(size, refs), out_shape=(out,) * 4, in...]
where the time goes in v3:
time: 25.9 us; the launch traced here: 25.7 us
  Pallas kernels  25 us (97%)
  between operations  0.64 us (2%)
    pallas_call x1, Pallas kernels, local(): pl.pallas_call(lambda *refs: kernel(size, refs), out_shape=(out,) * 4, in...  23 us
    pallas_call x1, Pallas kernels, local(): pl.pallas_call(flush, out_shape=(out,) * 4, in_specs=[pl.BlockSpec(memory...  1.98 us

profile of v3, /device:TPU:0, one launch (start us, length us, event | category | flops | bytes accessed | tf_op | source)
XLA Modules:
  0.0 25.7 jit_solution(392265771249940227)
XLA Ops:
  0.6 23.0 %shard_map.84 = (bf16[1,64,2048]{2,1,0:T(8,128)(2,1)}, bf16[1,64,2048]{2,1,0:T(8,128)(2,1)}, bf16[1,64,2048]{2,1,0:T(8,128)(2,1)}, bf16[1,64,2048]{2,1,0:T(8,128)(2,1)}) custom-call(s32[1,2048]{1,0:T(1,128)} %bitcast.1, bf16[1,64,2048]{2,1,0:T(8,128)(2,1)} %refs_1_.1, bf16[1,64,2048]{2,1,0:T(8,128)(2,1)} %refs_2_.1, bf16[1,64,2048]{2,1,0:T(8,128)(2,1)} %refs_3_.1, ...), custom_call_target="tpu_custom_call" | custom-call | flops 2000000000 | bytes 3000000 | tf_op jit(solution)/shard_map/pallas_call | solution.py:460
  23.7 2.0 %shard_map.85 = (bf16[1,64,2048]{2,1,0:T(8,128)(2,1)}, bf16[1,64,2048]{2,1,0:T(8,128)(2,1)}, bf16[1,64,2048]{2,1,0:T(8,128)(2,1)}, bf16[1,64,2048]{2,1,0:T(8,128)(2,1)}) custom-call(bf16[1,64,2048]{2,1,0:T(8,128)(2,1)} %get-tuple-element.8.refs_0_, bf16[1,64,2048]{2,1,0:T(8,128)(2,1)} %get-tuple-element.9.refs_1_, ...), custom_call_target="tpu_custom_call" | custom-call | tf_op jit(solution)/shard_map/pallas_call | solution.py:473
